TPU v7x, 128 devices: a whole 4x4x4 slice. The times are simulated.
128 devices in a mesh: dom: 8 (over z, core), grp: 16 (over x, y).
Axes of the slice: x: 4, y: 4, z: 4, core: 2. Of those that a mesh axis runs over, the one named last changes fastest.
Arguments:
- inputs: bfloat16 [393216, 256], P(('dom', 'grp')), may hold values from -6 to 6
- initial: bfloat16 [393216, 256], P(('dom', 'grp')), may hold values from -6 to 6
- history: bfloat16 [393216, 256], P(('dom', 'grp')), may hold values from -6 to 6
- upstream: bfloat16 [393216, 256], P(('dom', 'grp')), may hold values from -6 to 6
- weight: bfloat16 [256, 256], replicated, may hold values from -0.375 to 0.375
- tile_vals: bfloat16 [36864, 128, 128], P(('dom', 'grp')), may hold values from 0 to 0.088378906
- tile_row: int32 [36864], P(('dom', 'grp')), may hold values from 0 to 23
- tile_col: int32 [36864], P(('dom', 'grp')), may hold values from 0 to 47, as said below
- tile_count: int32 [128], P(('dom', 'grp')), may hold values from 48 to 288, as said below
- send_rows: int32 [8, 16, 128, 8], P('dom', 'grp'), may hold values from 0 to 3071
- cache_ask: int32 [8, 16, 8, 2], P('dom', 'grp'), may hold values from 0 to 23
Outputs:
- layer_out: bfloat16 [393216, 256], P(('dom', 'grp'))
- grad_inputs: float32 [393216, 256], P(('dom', 'grp'))
- grad_weight: float32 [256, 256], replicated
Inputs may be any that keep to these rules, and one draw needn't show every extreme that they name: `send_rows`: row numbers within the sending section. `cache_ask`: block numbers within the owning section. `tile_row`: row block within the section. `tile_col`: in each section's list the first 48 tiles name every column block once. `tile_count`: some section has exactly 288 live tiles.
All inputs are finite; a program needn't handle non-finite values.
Results may differ from a plain program's by a relative error of at most 0.0053.
Values may be sent and summed in bfloat16 or wider, within the bound.
A program may use at most 128 MiB of HBM per device.

v0:
```python
import math
import jax
import jax.numpy as jnp
from jax import lax
from jax.sharding import PartitionSpec as P

alpha_res = 0.1
beta_map = 0.4


def silu_slope(pre_act):
    squash = jax.nn.sigmoid(pre_act)
    return squash * (1.0 + pre_act * (1.0 - squash))


def turn_width(slot_count):
    for option_width in (96, 48, 32, 16, 8):
        return option_width
    return slot_count


def per_device(
    inputs,
    initial,
    history,
    upstream,
    weight,
    tile_vals,
    tile_row,
    tile_col,
    tile_count,
    send_rows,
    cache_ask,
):
    row_count, feature_dim = inputs.shape
    block_rows = tile_vals.shape[1]
    block_count = row_count // block_rows
    slot_count = tile_vals.shape[0]
    group_size = turn_width(slot_count)
    dom_count = lax.axis_size("dom")
    grp_count = lax.axis_size("grp")
    peer_count = dom_count * grp_count
    send_list = send_rows.reshape(peer_count, -1)
    per_peer = send_list.shape[1]
    ask_list = cache_ask.reshape(dom_count, -1)
    asked_per = ask_list.shape[1]
    outgoing = inputs[send_list.reshape(-1)].reshape(peer_count, per_peer, feature_dim)
    arrived = lax.all_to_all(outgoing, ("dom", "grp"), split_axis=0, concat_axis=0, tiled=True)
    arrived = arrived.reshape(peer_count * per_peer, feature_dim)
    wanted = lax.all_to_all(ask_list, "dom", split_axis=0, concat_axis=0, tiled=True)
    own_blocks = history.reshape(block_count, block_rows, feature_dim)
    served = own_blocks[wanted.reshape(-1)].reshape(dom_count, asked_per * block_rows, feature_dim)
    cached = lax.all_to_all(served, "dom", split_axis=0, concat_axis=0, tiled=True)
    cached = cached.reshape(dom_count * asked_per * block_rows, feature_dim)
    columns = jnp.concatenate([inputs, arrived, cached], axis=0)
    col_blocks = columns.reshape(-1, block_rows, feature_dim)
    column_total = col_blocks.shape[0]
    live_count = tile_count[0]
    turn_count = (live_count + group_size - 1) // group_size

    def turn_slices(turn_index):
        offset = turn_index * group_size
        tile_block = lax.dynamic_slice_in_dim(tile_vals, offset, group_size, 0)
        row_pick = lax.dynamic_slice_in_dim(tile_row, offset, group_size, 0)
        col_pick = lax.dynamic_slice_in_dim(tile_col, offset, group_size, 0)
        live_part = (offset + jnp.arange(group_size) < live_count).astype(jnp.float32)
        return (tile_block, row_pick, col_pick, live_part)

    def forward_turn(turn_index, totals):
        tile_block, row_pick, col_pick, live_part = turn_slices(turn_index)
        products = jnp.einsum(
            "tij,tjd->tid", tile_block, col_blocks[col_pick], preferred_element_type=jnp.float32
        )
        placing = (row_pick[:, None] == jnp.arange(block_count)[None, :]).astype(
            jnp.float32
        ) * live_part[:, None]
        return totals + jnp.einsum(
            "tr,tid->rid", placing, products, precision=lax.Precision.HIGHEST
        )

    gathered = lax.fori_loop(
        0, turn_count, forward_turn, jnp.zeros((block_count, block_rows, feature_dim), jnp.float32)
    )
    mixture = (1.0 - alpha_res) * gathered.reshape(
        row_count, feature_dim
    ) + alpha_res * initial.astype(jnp.float32)
    mixed_b = mixture.astype(jnp.bfloat16)
    pre_act = (1.0 - beta_map) * mixture + beta_map * jnp.dot(
        mixed_b, weight, preferred_element_type=jnp.float32
    )
    layer_out = jax.nn.silu(pre_act).astype(jnp.bfloat16)
    act_slope = upstream.astype(jnp.float32) * silu_slope(pre_act)
    slope_b = act_slope.astype(jnp.bfloat16)
    weight_part = lax.dot_general(
        mixed_b, slope_b, (((0,), (0,)), ((), ())), preferred_element_type=jnp.float32
    )
    through_weight = lax.dot_general(
        slope_b, weight, (((1,), (1,)), ((), ())), preferred_element_type=jnp.float32
    )
    back_grad = (
        (1.0 - alpha_res) * ((1.0 - beta_map) * act_slope + beta_map * through_weight)
    ).astype(jnp.bfloat16)
    back_blocks = back_grad.reshape(block_count, block_rows, feature_dim)

    def backward_turn(turn_index, totals):
        tile_block, row_pick, col_pick, live_part = turn_slices(turn_index)
        spread = jnp.einsum(
            "tji,tjd->tid", tile_block, back_blocks[row_pick], preferred_element_type=jnp.float32
        )
        onto_mask = (col_pick[:, None] == jnp.arange(column_total)[None, :]).astype(
            jnp.float32
        ) * live_part[:, None]
        return totals + jnp.einsum(
            "tc,tid->cid", onto_mask, spread, precision=lax.Precision.HIGHEST
        )

    column_grads = lax.fori_loop(
        0,
        turn_count,
        backward_turn,
        jnp.zeros((column_total, block_rows, feature_dim), jnp.float32),
    )
    fresh_blocks = peer_count * per_peer // block_rows
    own_grads = column_grads[:block_count].reshape(row_count, feature_dim)
    fresh_grads = (
        column_grads[block_count : block_count + fresh_blocks]
        .reshape(peer_count, per_peer, feature_dim)
        .astype(jnp.bfloat16)
    )
    returned = lax.all_to_all(fresh_grads, ("dom", "grp"), split_axis=0, concat_axis=0, tiled=True)
    returned = returned.reshape(peer_count * per_peer, feature_dim).astype(jnp.float32)
    grad_inputs = own_grads.at[send_list.reshape(-1)].add(returned)
    weight_total = lax.psum(weight_part, ("dom", "grp"))
    grad_weight = weight_total * (beta_map / math.sqrt(row_count * peer_count))
    return (layer_out, grad_inputs, grad_weight)


def solution(mesh):
    placed = (
        P(("dom", "grp"), None),
        P(("dom", "grp"), None),
        P(("dom", "grp"), None),
        P(("dom", "grp"), None),
        P(),
        P(("dom", "grp"), None, None),
        P(("dom", "grp")),
        P(("dom", "grp")),
        P(("dom", "grp")),
        P("dom", "grp", None, None),
        P("dom", "grp", None, None),
    )
    return jax.shard_map(
        per_device,
        mesh=mesh,
        in_specs=placed,
        out_specs=(P(("dom", "grp"), None), P(("dom", "grp"), None), P()),
        check_vma=False,
    )
```

profile of v0, /device:TPU:1, one launch (start us, length us, event | category | flops | bytes accessed | tf_op | source)
XLA Modules:
  0.0 450.1 jit_solution(1641534458222594287)
XLA Ops:
  7.2 0.0 copy-start
  7.2 1.5 copy.25
  8.6 6.8 %all-to-all-start.1 = ((s32[8,1,2]{2,1,0:T(1,128)}), s32[8,1,2]{2,1,0:T(1,128)S(1)}, u32[]{:S(2)}, u32[]{:S(2)}) async-start(s32[8,1,2]{2,1,0:T(1,128)} %copy.25), calls=%async_computation.1 | async-start | bytes 8192 | tf_op jit(solution)/shard_map/all_to_all | solution.py:50
  15.5 0.8 copy.24
  16.2 0.1 reshape_reshape.4
  16.4 0.0 copy-start.9
  16.4 0.6 copy-done.9
  17.0 6.2 %gather_fusion.2 = bf16[1024,256]{1,0:T(8,128)(2,1)} fusion(bf16[3072,256]{1,0:T(8,128)(2,1)} %param.15, s32[1024]{0:T(1024)S(1)} %broadcast_clamp_fusion), kind=kCustom, calls=%fused_computation.2 | custom fusion | bytes 1052672 | tf_op jit(solution)/shard_map/gather | solution.py:47
  23.2 0.0 all-to-all-done.1
  23.2 9.9 %all-to-all-start = ((bf16[128,8,256]{2,1,0:T(8,128)(2,1)}), bf16[128,8,256]{2,1,0:T(8,128)(2,1)}, u32[]{:S(2)}, u32[]{:S(2)}) async-start(bf16[128,8,256]{2,1,0:T(8,128)(2,1)} %bitcast.49), calls=%async_computation | async-start | bytes 1048576 | tf_op jit(solution)/shard_map/all_to_all | solution.py:48
  33.1 0.5 broadcast.141
  33.6 0.7 reduce.3
  34.3 0.1 reshape.119
  34.4 0.0 copy-done
  34.4 1.6 gather_fusion.3
  36.0 10.1 %all-to-all-done = bf16[128,8,256]{2,1,0:T(8,128)(2,1)} async-done(((bf16[128,8,256]{2,1,0:T(8,128)(2,1)}), bf16[128,8,256]{2,1,0:T(8,128)(2,1)}, u32[]{:S(2)}, u32[]{:S(2)}) %all-to-all-start) | async-done | bytes 524320 | tf_op jit(solution)/shard_map/all_to_all | solution.py:48
  46.1 4.8 %all-to-all-start.2 = ((bf16[8,256,256]{2,1,0:T(8,128)(2,1)}), bf16[8,256,256]{2,1,0:T(8,128)(2,1)S(1)}, u32[]{:S(2)}, u32[]{:S(2)}) async-start(bf16[8,256,256]{2,1,0:T(8,128)(2,1)} %bitcast.46), calls=%async_computation.2 | async-start | bytes 2097152 | tf_op jit(solution)/shard_map/all_to_all | solution.py:53
  51.6 14.4 %all-to-all-done.2 = bf16[8,256,256]{2,1,0:T(8,128)(2,1)S(1)} async-done(((bf16[8,256,256]{2,1,0:T(8,128)(2,1)}), bf16[8,256,256]{2,1,0:T(8,128)(2,1)S(1)}, u32[]{:S(2)}, u32[]{:S(2)}) %all-to-all-start.2) | async-done | bytes 1048608 | tf_op jit(solution)/shard_map/all_to_all | solution.py:53
  66.0 10.3 %pad_maximum_fusion = bf16[6144,256]{1,0:T(8,128)(2,1)} fusion(bf16[2048,256]{1,0:T(8,128)(2,1)S(1)} %bitcast.47, bf16[1024,256]{1,0:T(8,128)(2,1)} %bitcast.5, bf16[3072,256]{1,0:T(8,128)(2,1)S(1)} %copy-done.6), kind=kLoop, calls=%fused_computation.43 | loop fusion | flops 9437184 | bytes 6291456 | tf_op jit(solution)/shard_map/concatenate | solution.py:55
  76.3 1.9 broadcast_in_dim.12
  78.2 30.3 %while.20 = (s32[]{:T(128)}, f32[24,128,256]{2,0,1:T(8,128)}, s32[]{:T(128)}, s32[288]{0:T(512)S(1)}, s32[]{:T(128)}, /*index=5*/bf16[288,128,128]{2,1,0:T(8,128...) while((s32[]{:T(128)}, f32[24,128,256]{2,0,1:T(8,128)}, ...), condition=%wide.region_1.2_spmd, body=%wide.region_0.1_spmd.sunk | while | flops 1712068736 | bytes 78650992 | solution.py:81
  78.4 0.7 compare_convert_fusion.4
  79.0 0.1 compare_select_fusion.6
  79.1 0.1 dynamic_slice.32
  79.2 7.9 %gather_fusion = bf16[96,128,256]{2,1,0:T(8,128)(2,1)} fusion(bf16[48,128,256]{2,1,0:T(8,128)(2,1)} %get-tuple-element.264, s32[1024]{0:T(1024)S(1)} %pad_clamp_fusion.5), kind=kCustom, calls=%fused_computation.clone.1 | custom fusion | bytes 12583296 | tf_op jit(solution)/shard_map/while/body/gather | solution.py:72
  87.1 5.7 %fusion.61 = f32[96,128,256]{2,1,0:T(8,128)S(1)} fusion(bf16[96,128,256]{2,1,0:T(8,128)(2,1)} %gather_fusion, bf16[288,128,128]{2,1,0:T(8,128)(2,1)} %get-tuple-element.262, s32[]{:T(128)S(6)} %select_n.56), kind=kOutput, calls=%fused_computation.7.clone.1 | convolution fusion | flops 805306368 | bytes 22020100 | tf_op jit(solution)/shard_map/while/body/tij,tjd->tid/dot_general | solution.py:71
  92.8 13.7 %fusion.62 = f32[24,128,256]{2,0,1:T(8,128)S(1)} fusion(f32[24,128,256]{2,0,1:T(8,128)S(1)} %copy-done.4, f32[96,128,256]{2,1,0:T(8,128)S(1)} %fusion.61, f32[96]{0:T(128)S(1)} %compare_convert_fusion.4, s32[96]{0:T(128)S(1)} %dynamic_slice.32), kind=kOutput, calls=%fused_computation.9.clone.1 | convolution fusion | flops 906760704 | bytes 18875136 | tf_op jit(solution)/shard_map/while/body/tr,tid->rid/dot_general | solution.py:77
  106.5 0.0 copy-start.5
  106.5 1.7 copy-done.5
  108.5 2.2 broadcast_multiply_fusion
  110.7 0.0 copy-start.8
  110.7 1.0 copy.26
  111.7 0.4 copy-done.8
  112.1 0.4 bitcast_add_fusion
  112.5 0.5 copy-done.12
  113.0 2.3 multiply_convert_fusion
  115.3 0.2 copy-done.10
  115.5 2.9 fusion.31
  118.5 3.5 broadcast_in_dim.13
  122.0 30.3 %while.21 = (s32[]{:T(128)}, f32[48,128,256]{2,0,1:T(8,128)}, s32[]{:T(128)}, s32[288]{0:T(512)S(1)}, s32[]{:T(128)}, /*index=5*/bf16[288,128,128]{2,1,0:T(8,128...) while((s32[]{:T(128)}, f32[48,128,256]{2,0,1:T(8,128)}, ...), condition=%wide.region_3.4_spmd, body=%wide.region_2.3_spmd.sunk | while | flops 2618829312 | bytes 110108272 | solution.py:117
  122.1 0.7 compare_convert_fusion.5
  122.8 0.1 compare_select_fusion.7
  122.9 0.1 dynamic_slice.35
  122.9 5.9 %gather_fusion.1 = bf16[96,128,256]{2,1,0:T(8,128)(2,1)} fusion(bf16[24,128,256]{2,1,0:T(8,128)(2,1)S(1)} %get-tuple-element.300, s32[1024]{0:T(1024)S(1)} %pad_clamp_fusion.6), kind=kCustom, calls=%fused_computation.1.clone.1 | custom fusion | bytes 12583296 | tf_op jit(solution)/shard_map/while/body/gather | solution.py:108
  128.9 5.7 %fusion.67 = f32[96,128,256]{2,1,0:T(8,128)S(1)} fusion(bf16[96,128,256]{2,1,0:T(8,128)(2,1)} %gather_fusion.1, bf16[288,128,128]{2,1,0:T(8,128)(2,1)} %get-tuple-element.298, s32[]{:T(128)S(6)} %select_n.58), kind=kOutput, calls=%fused_computation.23.clone.1 | convolution fusion | flops 805306368 | bytes 22020100 | tf_op jit(solution)/shard_map/while/body/tji,tjd->tid/dot_general | solution.py:107
  134.6 0.0 copy-done.2
  134.6 14.8 %fusion.68 = f32[48,128,256]{2,0,1:T(8,128)S(1)} fusion(f32[48,128,256]{2,0,1:T(8,128)S(1)} %copy-done.2, f32[96,128,256]{2,1,0:T(8,128)S(1)} %fusion.67, f32[96]{0:T(128)S(1)} %compare_convert_fusion.5, s32[96]{0:T(128)S(1)} %dynamic_slice.35), kind=kOutput, calls=%fused_computation.25.clone.1 | convolution fusion | flops 1813521408 | bytes 25166592 | tf_op jit(solution)/shard_map/while/body/tc,tid->cid/dot_general | solution.py:113
  149.4 0.0 copy-start.3
  149.4 2.7 copy-done.3
  152.2 0.0 copy-start.11
  152.3 6.2 %copy.29 = bf16[48,128,256]{2,1,0:T(8,128)(2,1)S(1)} copy(f32[48,128,256]{2,0,1:T(8,128)} %get-tuple-element.90) | data formatting | bytes 9437184 | tf_op jit(solution)/shard_map/while | solution.py:117
  158.5 0.8 slice.19
  159.3 123.0 %all-to-all-start.3 = ((bf16[128,8,256]{2,1,0:T(8,128)(2,1)}), bf16[128,8,256]{2,1,0:T(8,128)(2,1)S(1)}, u32[]{:S(2)}, u32[]{:S(2)}) async-start(bf16[128,8,256]{2,1,0:T(8,128)(2,1)} %bitcast.15), calls=%async_computation.3 | async-start | bytes 1048576 | tf_op jit(solution)/shard_map/all_to_all | solution.py:130
  282.3 0.0 all-reduce.2.cloned.1.call-start
  282.4 5.0 %fusion.34 = f32[256,256]{1,0:T(8,128)} fusion(f32[3072,256]{1,0:T(8,128)} %copy-done.7, f32[3072,256]{1,0:T(8,128)} %copy-done.15, bf16[3072,256]{1,0:T(8,128)(2,1)S(1)} %copy-done.11), kind=kOutput, calls=%fused_computation.52 | convolution fusion | flops 411303936 | bytes 8126464 | tf_op jit(solution)/shard_map/dot_general | solution.py:94
  287.4 0.0 all-reduce.2.cloned.1.call-update
  287.4 2.1 slice.7
  289.5 0.0 copy-start.1
  289.6 2.6 copy.28
  292.2 139.4 %all-reduce.2.cloned.1.call-done = f32[256,256]{1,0:T(8,128)} async-done(((f32[256,256]{1,0:T(8,128)}), f32[256,256]{1,0:T(8,128)}) %all-reduce.2.cloned.1.call-update) | async-done | bytes 262160 | tf_op jit(solution)/shard_map/psum | solution.py:133
  431.6 1.7 broadcast_multiply_fusion.1
  433.3 0.0 all-to-all-done.3
  433.3 9.7 %scatter_custom_fusion = f32[3072,256]{1,0:T(8,128)} fusion(f32[3072,256]{1,0:T(8,128)} %bitcast.48, s32[1024]{0:T(1024)} %bitcast.51, bf16[128,8,256]{2,1,0:T(8,128)(2,1)S(1)} %all-to-all-done.3), kind=kCustom, calls=%fused_computation.50 | custom fusion | flops 524288 | bytes 3670016 | tf_op jit(solution)/shard_map/scatter-add | solution.py:132
  443.0 0.0 copy-done.1
  (22 shorter events, 0.1 us)
Async XLA Ops:
  7.2 27.2 %copy-start = (bf16[3072,256]{1,0:T(8,128)(2,1)S(1)}, bf16[3072,256]{1,0:T(8,128)(2,1)}, u32[]{:S(2)}) copy-start(bf16[3072,256]{1,0:T(8,128)(2,1)} %param.17) | copy-start | bytes 4718596
  8.6 14.5 %all-to-all-start.1 = ((s32[8,1,2]{2,1,0:T(1,128)}), s32[8,1,2]{2,1,0:T(1,128)S(1)}, u32[]{:S(2)}, u32[]{:S(2)}) async-start(s32[8,1,2]{2,1,0:T(1,128)} %copy.25), calls=%async_computation.1 | async-start | bytes 8192 | tf_op jit(solution)/shard_map/all_to_all | solution.py:50
  16.4 0.6 copy-start.9
  23.2 42.9 %copy-start.6 = (bf16[3072,256]{1,0:T(8,128)(2,1)S(1)}, bf16[3072,256]{1,0:T(8,128)(2,1)}, u32[]{:S(2)}) copy-start(bf16[3072,256]{1,0:T(8,128)(2,1)} %param.15) | copy-start | bytes 4718596
  23.2 22.9 %all-to-all-start = ((bf16[128,8,256]{2,1,0:T(8,128)(2,1)}), bf16[128,8,256]{2,1,0:T(8,128)(2,1)}, u32[]{:S(2)}, u32[]{:S(2)}) async-start(bf16[128,8,256]{2,1,0:T(8,128)(2,1)} %bitcast.49), calls=%async_computation | async-start | bytes 1048576 | tf_op jit(solution)/shard_map/all_to_all | solution.py:48
  46.1 19.9 %all-to-all-start.2 = ((bf16[8,256,256]{2,1,0:T(8,128)(2,1)}), bf16[8,256,256]{2,1,0:T(8,128)(2,1)S(1)}, u32[]{:S(2)}, u32[]{:S(2)}) async-start(bf16[8,256,256]{2,1,0:T(8,128)(2,1)} %bitcast.46), calls=%async_computation.2 | async-start | bytes 2097152 | tf_op jit(solution)/shard_map/all_to_all | solution.py:53
  76.3 1.9 copy-start.13
  76.3 1.9 copy-start.14
  87.1 5.7 %copy-start.4 = (f32[24,128,256]{2,0,1:T(8,128)S(1)}, f32[24,128,256]{2,0,1:T(8,128)}, u32[]{:S(2)}) copy-start(f32[24,128,256]{2,0,1:T(8,128)} %get-tuple-element.246) | copy-start | bytes 9437188 | tf_op jit(solution)/shard_map/while
  106.5 1.7 copy-start.5
  110.7 1.4 copy-start.8
  112.1 0.9 copy-start.12
  113.0 2.3 copy-start.7
  113.0 2.5 copy-start.10
  115.3 3.2 copy-start.15
  128.9 5.7 %copy-start.2 = (f32[48,128,256]{2,0,1:T(8,128)S(1)}, f32[48,128,256]{2,0,1:T(8,128)}, u32[]{:S(2)}) copy-start(f32[48,128,256]{2,0,1:T(8,128)} %get-tuple-element.282) | copy-start | bytes 18874372 | tf_op jit(solution)/shard_map/while
  149.4 2.7 copy-start.3
  152.2 130.1 %copy-start.11 = (bf16[3072,256]{1,0:T(8,128)(2,1)S(1)}, bf16[3072,256]{1,0:T(8,128)(2,1)}, u32[]{:S(2)}) copy-start(bf16[3072,256]{1,0:T(8,128)(2,1)} %param.18) | copy-start | bytes 4718596
  159.3 273.9 %all-to-all-start.3 = ((bf16[128,8,256]{2,1,0:T(8,128)(2,1)}), bf16[128,8,256]{2,1,0:T(8,128)(2,1)S(1)}, u32[]{:S(2)}, u32[]{:S(2)}) async-start(bf16[128,8,256]{2,1,0:T(8,128)(2,1)} %bitcast.15), calls=%async_computation.3 | async-start | bytes 1048576 | tf_op jit(solution)/shard_map/all_to_all | solution.py:130
  282.3 149.3 %all-reduce.2.cloned.1.call-start = ((), (), s32[]{:S(2)}) async-start(), calls=%async_computation.4 | async-start | bytes 524288 | tf_op jit(solution)/shard_map/psum | solution.py:133
  289.5 153.5 %copy-start.1 = (bf16[3072,256]{1,0:T(8,128)(2,1)S(1)}, bf16[3072,256]{1,0:T(8,128)(2,1)}, u32[]{:S(2)}) copy-start(bf16[3072,256]{1,0:T(8,128)(2,1)} %param.17) | copy-start | bytes 4718596
Sparse Core Ops, SparseCore 0:
  288.5 143.0 all-reduce.1
where the time goes:
time: 456 us; the launch traced here: 450 us
  waiting for transfers between devices  164 us (36%)
  starting transfers between devices  145 us (32%)
  matrix products  50.1 us (11%)
  local copies, waits for them, and re-layouts  48.9 us (11%)
  other arithmetic  26.4 us (6%)
  between operations  15.1 us (3%)
    psum x1, waiting for transfers between devices, per_device(): weight_total = lax.psum(weight_part, ('dom', 'grp'))  139 us
    all_to_all x1, starting transfers between devices, per_device(): lax.all_to_all(fresh_grads, ('dom', 'grp'), split_axis=0, concat_axis=0,...  123 us
    dot_general x1, matrix products, backward_turn(): jnp.einsum('tc,tid->cid', onto_mask, spread, precision=lax.Precision.HIGH...  14.8 us
    all_to_all x1, waiting for transfers between devices, per_device(): lax.all_to_all(served, 'dom', split_axis=0, concat_axis=0, tiled=True)  14.4 us
    dot_general x1, matrix products, forward_turn(): jnp.einsum('tr,tid->rid', placing, products, precision=lax.Precision.HIGH...  13.7 us
    concatenate x1, other arithmetic, per_device(): columns = jnp.concatenate([inputs, arrived, cached], axis=0)  10.3 us
    all_to_all x1, waiting for transfers between devices, per_device(): lax.all_to_all(outgoing, ('dom', 'grp'), split_axis=0, concat_axis=0, til...  10.1 us
    all_to_all x1, starting transfers between devices, per_device(): lax.all_to_all(outgoing, ('dom', 'grp'), split_axis=0, concat_axis=0, til...  9.95 us
  transfers between devices with their start and end apart: 5, of which 3 were waited for; matrix products, arithmetic and copies ran while one was open for 5% of the time, Pallas kernels for 0%

commit v1 on v0

--- a/solution.py
+++ b/solution.py
@@ -130,7 +130,7 @@
     returned = lax.all_to_all(fresh_grads, ("dom", "grp"), split_axis=0, concat_axis=0, tiled=True)
     returned = returned.reshape(peer_count * per_peer, feature_dim).astype(jnp.float32)
     grad_inputs = own_grads.at[send_list.reshape(-1)].add(returned)
-    weight_total = lax.psum(weight_part, ("dom", "grp"))
+    weight_total = jnp.sum(lax.all_gather(weight_part, ("dom", "grp")), axis=0)
     grad_weight = weight_total * (beta_map / math.sqrt(row_count * peer_count))
     return (layer_out, grad_inputs, grad_weight)
 

time: 456 us -> 338 us (0.74)
  waiting for transfers between devices: 164 us -> 33.2 us
  other arithmetic: 26.4 us -> 37.6 us
    psum x1 -> x0, waiting for transfers between devices: 139 us -> none  [per_device(): weight_total = lax.psum(weight_part, ('dom', 'grp'))]
    reduce_sum x0 -> x1, other arithmetic: none -> 12.1 us  [per_device(): weight_total = jnp.sum(lax.all_gather(weight_part, ('dom', 'grp')), axis=0)]
    all_to_all x1, waiting for transfers between devices: 0.01 us -> 8.59 us  [per_device(): lax.all_to_all(fresh_grads, ('dom', 'grp'), split_axis=0, concat_axis=0,...]
  transfers between devices with their start and end apart: 5 -> 5, of which waited for: 3 -> 3; matrix products, arithmetic and copies ran while one was open for 5% -> 20% of each run, Pallas kernels for 0% -> 0%
where the time goes in v1:
time: 338 us; the launch traced here: 332 us
  starting transfers between devices  145 us (43%)
  local copies, waits for them, and re-layouts  50.2 us (15%)
  matrix products  49.9 us (15%)
  other arithmetic  37.6 us (11%)
  waiting for transfers between devices  33.2 us (10%)
  between operations  15 us (4%)
    all_to_all x1, starting transfers between devices, per_device(): lax.all_to_all(fresh_grads, ('dom', 'grp'), split_axis=0, concat_axis=0,...  124 us
    dot_general x1, matrix products, backward_turn(): jnp.einsum('tc,tid->cid', onto_mask, spread, precision=lax.Precision.HIGH...  14.8 us
    all_to_all x1, waiting for transfers between devices, per_device(): lax.all_to_all(served, 'dom', split_axis=0, concat_axis=0, tiled=True)  14.4 us
    dot_general x1, matrix products, forward_turn(): jnp.einsum('tr,tid->rid', placing, products, precision=lax.Precision.HIGH...  13.7 us
    reduce_sum x1, other arithmetic, per_device(): weight_total = jnp.sum(lax.all_gather(weight_part, ('dom', 'grp')), axis=0)  12.1 us
    concatenate x1, other arithmetic, per_device(): columns = jnp.concatenate([inputs, arrived, cached], axis=0)  10.3 us
    all_to_all x1, waiting for transfers between devices, per_device(): lax.all_to_all(outgoing, ('dom', 'grp'), split_axis=0, concat_axis=0, til...  10.1 us
    all_to_all x1, starting transfers between devices, per_device(): lax.all_to_all(outgoing, ('dom', 'grp'), split_axis=0, concat_axis=0, til...  9.95 us
  transfers between devices with their start and end apart: 5, of which 3 were waited for; matrix products, arithmetic and copies ran while one was open for 20% of the time, Pallas kernels for 0%

profile of v1, /device:TPU:1, one launch (start us, length us, event | category | flops | bytes accessed | tf_op | source)
XLA Modules:
  0.0 332.2 jit_solution(13790550390070972307)
XLA Ops:
  7.2 0.0 copy-start
  7.2 1.5 copy.25
  8.6 6.8 %all-to-all-start.1 = ((s32[8,1,2]{2,1,0:T(1,128)}), s32[8,1,2]{2,1,0:T(1,128)S(1)}, u32[]{:S(2)}, u32[]{:S(2)}) async-start(s32[8,1,2]{2,1,0:T(1,128)} %copy.25), calls=%async_computation.1 | async-start | bytes 8192 | tf_op jit(solution)/shard_map/all_to_all | solution.py:50
  15.5 0.8 copy.24
  16.2 0.1 reshape_reshape.4
  16.4 0.0 copy-start.7
  16.4 0.6 copy-done.7
  17.0 6.2 %gather_fusion.2 = bf16[1024,256]{1,0:T(8,128)(2,1)} fusion(bf16[3072,256]{1,0:T(8,128)(2,1)} %param.15, s32[1024]{0:T(1024)S(1)} %broadcast_clamp_fusion), kind=kCustom, calls=%fused_computation.2 | custom fusion | bytes 1052672 | tf_op jit(solution)/shard_map/gather | solution.py:47
  23.2 0.0 all-to-all-done.1
  23.2 9.9 %all-to-all-start = ((bf16[128,8,256]{2,1,0:T(8,128)(2,1)}), bf16[128,8,256]{2,1,0:T(8,128)(2,1)}, u32[]{:S(2)}, u32[]{:S(2)}) async-start(bf16[128,8,256]{2,1,0:T(8,128)(2,1)} %bitcast.53), calls=%async_computation | async-start | bytes 1048576 | tf_op jit(solution)/shard_map/all_to_all | solution.py:48
  33.1 0.5 broadcast.141
  33.7 0.7 reduce.3
  34.3 0.1 reshape.119
  34.4 0.0 copy-done
  34.4 1.6 gather_fusion.3
  36.0 10.1 %all-to-all-done = bf16[128,8,256]{2,1,0:T(8,128)(2,1)} async-done(((bf16[128,8,256]{2,1,0:T(8,128)(2,1)}), bf16[128,8,256]{2,1,0:T(8,128)(2,1)}, u32[]{:S(2)}, u32[]{:S(2)}) %all-to-all-start) | async-done | bytes 524320 | tf_op jit(solution)/shard_map/all_to_all | solution.py:48
  46.1 4.8 %all-to-all-start.2 = ((bf16[8,256,256]{2,1,0:T(8,128)(2,1)}), bf16[8,256,256]{2,1,0:T(8,128)(2,1)S(1)}, u32[]{:S(2)}, u32[]{:S(2)}) async-start(bf16[8,256,256]{2,1,0:T(8,128)(2,1)} %bitcast.50), calls=%async_computation.2 | async-start | bytes 2097152 | tf_op jit(solution)/shard_map/all_to_all | solution.py:53
  50.9 0.0 all-gather.3.cloned.1.call-start
  51.6 14.4 %all-to-all-done.2 = bf16[8,256,256]{2,1,0:T(8,128)(2,1)S(1)} async-done(((bf16[8,256,256]{2,1,0:T(8,128)(2,1)}), bf16[8,256,256]{2,1,0:T(8,128)(2,1)S(1)}, u32[]{:S(2)}, u32[]{:S(2)}) %all-to-all-start.2) | async-done | bytes 1048608 | tf_op jit(solution)/shard_map/all_to_all | solution.py:53
  66.0 0.0 copy-done.5
  66.0 10.3 %pad_maximum_fusion = bf16[6144,256]{1,0:T(8,128)(2,1)} fusion(bf16[2048,256]{1,0:T(8,128)(2,1)S(1)} %bitcast.51, bf16[1024,256]{1,0:T(8,128)(2,1)} %bitcast.5, bf16[3072,256]{1,0:T(8,128)(2,1)S(1)} %copy-done.5), kind=kLoop, calls=%fused_computation.43 | loop fusion | flops 9437184 | bytes 6291456 | tf_op jit(solution)/shard_map/concatenate | solution.py:55
  76.3 1.9 broadcast_in_dim.12
  78.2 0.0 copy-done.10
  78.2 0.0 copy-done.11
  78.2 30.3 %while.20 = (s32[]{:T(128)}, f32[24,128,256]{2,0,1:T(8,128)}, s32[]{:T(128)}, s32[288]{0:T(512)S(1)}, s32[]{:T(128)}, /*index=5*/bf16[288,128,128]{2,1,0:T(8,128...) while((s32[]{:T(128)}, f32[24,128,256]{2,0,1:T(8,128)}, ...), condition=%wide.region_1.2_spmd, body=%wide.region_0.1_spmd.sunk | while | flops 1712068736 | bytes 78651000 | solution.py:81
  78.4 0.1 compare_select_fusion.6
  78.5 7.9 %gather_fusion = bf16[96,128,256]{2,1,0:T(8,128)(2,1)} fusion(bf16[48,128,256]{2,1,0:T(8,128)(2,1)} %get-tuple-element.264, s32[1024]{0:T(1024)S(1)} %pad_clamp_fusion.5), kind=kCustom, calls=%fused_computation.clone.1 | custom fusion | bytes 12583296 | tf_op jit(solution)/shard_map/while/body/gather | solution.py:72
  86.4 5.7 %fusion.61 = f32[96,128,256]{2,1,0:T(8,128)S(1)} fusion(bf16[96,128,256]{2,1,0:T(8,128)(2,1)} %gather_fusion, bf16[288,128,128]{2,1,0:T(8,128)(2,1)} %get-tuple-element.262, s32[]{:T(128)S(6)} %select_n.56), kind=kOutput, calls=%fused_computation.7.clone.1 | convolution fusion | flops 805306368 | bytes 22020100 | tf_op jit(solution)/shard_map/while/body/tij,tjd->tid/dot_general | solution.py:71
  92.0 0.7 compare_convert_fusion.4
  92.7 0.1 dynamic_slice.32
  92.8 13.7 %fusion.62 = f32[24,128,256]{2,0,1:T(8,128)S(1)} fusion(f32[24,128,256]{2,0,1:T(8,128)S(1)} %copy-done.3, f32[96,128,256]{2,1,0:T(8,128)S(1)} %fusion.61, f32[96]{0:T(128)S(1)} %compare_convert_fusion.4, s32[96]{0:T(128)S(1)} %dynamic_slice.32), kind=kOutput, calls=%fused_computation.9.clone.1 | convolution fusion | flops 906760704 | bytes 18875136 | tf_op jit(solution)/shard_map/while/body/tr,tid->rid/dot_general | solution.py:77
  106.4 0.0 copy-start.4
  106.5 1.7 copy-done.4
  108.5 2.2 broadcast_multiply_fusion
  110.7 0.0 copy-start.6
  110.7 1.0 copy.26
  111.7 0.4 copy-done.6
  112.1 0.4 bitcast_add_fusion
  112.5 0.5 copy-done.9
  113.0 2.3 multiply_convert_fusion
  115.3 1.7 copy-done.12
  117.0 2.2 fusion.34
  119.2 0.0 all-gather.3.cloned.1.call-update
  119.2 5.6 %fusion.31 = bf16[3072,256]{1,0:T(8,128)(2,1)S(1)} fusion(bf16[256,256]{1,0:T(8,128)(2,1)S(1)} %copy-done.9, f32[3072,256]{1,0:T(8,128)} %copy-done.12, bf16[3072,256]{1,0:T(8,128)(2,1)S(1)} %copy-done.8), kind=kOutput, calls=%fused_computation.42 | convolution fusion | flops 421527552 | bytes 6422528 | tf_op jit(solution)/shard_map/dot_general | solution.py:97
  124.8 3.4 %broadcast_in_dim.13 = f32[48,128,256]{2,0,1:T(8,128)} broadcast(f32[]{:T(128)} %constant.39.clone.1), dimensions={} | broadcast | bytes 6291460 | tf_op jit(solution)/shard_map/broadcast_in_dim | solution.py:121
  128.3 30.2 %while.21 = (s32[]{:T(128)}, f32[48,128,256]{2,0,1:T(8,128)}, s32[]{:T(128)}, s32[288]{0:T(512)S(1)}, s32[]{:T(128)}, /*index=5*/bf16[288,128,128]{2,1,0:T(8,128...) while((s32[]{:T(128)}, f32[48,128,256]{2,0,1:T(8,128)}, ...), condition=%wide.region_3.4_spmd, body=%wide.region_2.3_spmd.sunk | while | flops 2618829312 | bytes 103816832 | solution.py:117
  128.4 0.1 compare_select_fusion.7
  128.5 5.9 %gather_fusion.1 = bf16[96,128,256]{2,1,0:T(8,128)(2,1)} fusion(bf16[24,128,256]{2,1,0:T(8,128)(2,1)S(1)} %get-tuple-element.300, s32[1024]{0:T(1024)S(1)} %pad_clamp_fusion.6), kind=kCustom, calls=%fused_computation.1.clone.1 | custom fusion | bytes 12583296 | tf_op jit(solution)/shard_map/while/body/gather | solution.py:108
  134.4 5.7 %fusion.67 = f32[96,128,256]{2,1,0:T(8,128)S(1)} fusion(bf16[96,128,256]{2,1,0:T(8,128)(2,1)} %gather_fusion.1, bf16[288,128,128]{2,1,0:T(8,128)(2,1)} %get-tuple-element.298, s32[]{:T(128)S(6)} %select_n.58), kind=kOutput, calls=%fused_computation.23.clone.1 | convolution fusion | flops 805306368 | bytes 22020100 | tf_op jit(solution)/shard_map/while/body/tji,tjd->tid/dot_general | solution.py:107
  140.2 0.7 compare_convert_fusion.5
  140.8 0.1 dynamic_slice.35
  140.9 0.0 slice-done.1
  140.9 14.8 %fusion.68 = f32[48,128,256]{2,0,1:T(8,128)S(1)} fusion(f32[48,128,256]{2,0,1:T(8,128)S(1)} %bitcast.48, f32[96,128,256]{2,1,0:T(8,128)S(1)} %fusion.67, f32[96]{0:T(128)S(1)} %compare_convert_fusion.5, s32[96]{0:T(128)S(1)} %dynamic_slice.35), kind=kOutput, calls=%fused_computation.25.clone.1 | convolution fusion | flops 1813521408 | bytes 25166592 | tf_op jit(solution)/shard_map/while/body/tc,tid->cid/dot_general | solution.py:113
  155.7 2.6 copy-done.2
  158.5 6.1 %copy.29 = bf16[48,128,256]{2,1,0:T(8,128)(2,1)S(1)} copy(f32[48,128,256]{2,0,1:T(8,128)} %get-tuple-element.90) | data formatting | bytes 9437184 | tf_op jit(solution)/shard_map/while | solution.py:117
  164.6 0.9 slice.19
  165.5 123.8 %all-to-all-start.3 = ((bf16[128,8,256]{2,1,0:T(8,128)(2,1)}), bf16[128,8,256]{2,1,0:T(8,128)(2,1)S(1)}, u32[]{:S(2)}, u32[]{:S(2)}) async-start(bf16[128,8,256]{2,1,0:T(8,128)(2,1)} %bitcast.15), calls=%async_computation.3 | async-start | bytes 1048576 | tf_op jit(solution)/shard_map/all_to_all | solution.py:130
  289.3 2.1 slice.7
  291.4 2.6 copy.28
  294.0 8.6 %all-to-all-done.3 = bf16[128,8,256]{2,1,0:T(8,128)(2,1)S(1)} async-done(((bf16[128,8,256]{2,1,0:T(8,128)(2,1)}), bf16[128,8,256]{2,1,0:T(8,128)(2,1)S(1)}, u32[]{:S(2)}, u32[]{:S(2)}) %all-to-all-start.3) | async-done | bytes 524320 | tf_op jit(solution)/shard_map/all_to_all | solution.py:130
  302.6 9.7 %scatter_custom_fusion = f32[3072,256]{1,0:T(8,128)} fusion(f32[3072,256]{1,0:T(8,128)} %bitcast.52, s32[1024]{0:T(1024)} %bitcast.55, bf16[128,8,256]{2,1,0:T(8,128)(2,1)S(1)} %all-to-all-done.3), kind=kCustom, calls=%fused_computation.50 | custom fusion | flops 524288 | bytes 3670016 | tf_op jit(solution)/shard_map/scatter-add | solution.py:132
  312.4 12.1 %reduce_sum.9 = f32[256,256]{1,0:T(8,128)S(1)} reduce(f32[128,256,256]{2,1,0:T(8,128)} %bitcast.49, f32[]{:T(128)} %constant.39.clone.1), dimensions={0}, to_apply=%region_5.6 | reduce | flops 8323072 | bytes 33816580 | tf_op jit(solution)/shard_map/reduce_sum | solution.py:133
  324.4 0.7 broadcast_multiply_fusion.1
  325.2 0.0 copy-done.1
  (22 shorter events, 0.1 us)
Async XLA Ops:
  7.2 27.3 %copy-start = (bf16[3072,256]{1,0:T(8,128)(2,1)S(1)}, bf16[3072,256]{1,0:T(8,128)(2,1)}, u32[]{:S(2)}) copy-start(bf16[3072,256]{1,0:T(8,128)(2,1)} %param.17) | copy-start | bytes 4718596
  8.6 14.5 %all-to-all-start.1 = ((s32[8,1,2]{2,1,0:T(1,128)}), s32[8,1,2]{2,1,0:T(1,128)S(1)}, u32[]{:S(2)}, u32[]{:S(2)}) async-start(s32[8,1,2]{2,1,0:T(1,128)} %copy.25), calls=%async_computation.1 | async-start | bytes 8192 | tf_op jit(solution)/shard_map/all_to_all | solution.py:50
  16.4 0.6 copy-start.7
  23.2 42.9 %copy-start.5 = (bf16[3072,256]{1,0:T(8,128)(2,1)S(1)}, bf16[3072,256]{1,0:T(8,128)(2,1)}, u32[]{:S(2)}) copy-start(bf16[3072,256]{1,0:T(8,128)(2,1)} %param.15) | copy-start | bytes 4718596
  23.2 22.9 %all-to-all-start = ((bf16[128,8,256]{2,1,0:T(8,128)(2,1)}), bf16[128,8,256]{2,1,0:T(8,128)(2,1)}, u32[]{:S(2)}, u32[]{:S(2)}) async-start(bf16[128,8,256]{2,1,0:T(8,128)(2,1)} %bitcast.53), calls=%async_computation | async-start | bytes 1048576 | tf_op jit(solution)/shard_map/all_to_all | solution.py:48
  46.1 19.9 %all-to-all-start.2 = ((bf16[8,256,256]{2,1,0:T(8,128)(2,1)}), bf16[8,256,256]{2,1,0:T(8,128)(2,1)S(1)}, u32[]{:S(2)}, u32[]{:S(2)}) async-start(bf16[8,256,256]{2,1,0:T(8,128)(2,1)} %bitcast.50), calls=%async_computation.2 | async-start | bytes 2097152 | tf_op jit(solution)/shard_map/all_to_all | solution.py:53
  50.9 261.4 %all-gather.3.cloned.1.call-start = ((), (), s32[]{:S(2)}) async-start(), calls=%async_computation.4 | async-start | bytes 33816576 | tf_op jit(solution)/shard_map/all_gather | solution.py:133
  76.3 1.9 copy-start.10
  76.3 1.9 copy-start.11
  86.4 6.4 %copy-start.3 = (f32[24,128,256]{2,0,1:T(8,128)S(1)}, f32[24,128,256]{2,0,1:T(8,128)}, u32[]{:S(2)}) copy-start(f32[24,128,256]{2,0,1:T(8,128)} %get-tuple-element.246) | copy-start | bytes 9437188 | tf_op jit(solution)/shard_map/while
  106.4 1.7 copy-start.4
  110.7 1.4 copy-start.6
  112.1 0.9 copy-start.9
  113.0 4.0 %copy-start.8 = (bf16[3072,256]{1,0:T(8,128)(2,1)S(1)}, bf16[3072,256]{1,0:T(8,128)(2,1)}, u32[]{:S(2)}) copy-start(bf16[3072,256]{1,0:T(8,128)(2,1)} %param.18) | copy-start | bytes 4718596
  115.3 1.7 copy-start.12
  134.4 6.5 %slice-start = ((s8[6291456]{0:T(1024)(128)(4,1)}), s8[4194304]{0:T(1024)(128)(4,1)S(1)}, s32[]{:S(2)}) async-start(s8[6291456]{0:T(1024)(128)(4,1)} %bitcast.47), calls=%async_computation.5 | async-start | bytes 8388608 | tf_op jit(solution)/shard_map/while
  134.4 6.5 %slice-start.1 = ((s8[6291456]{0:T(1024)(128)(4,1)}), s8[2097152]{0:T(1024)(128)(4,1)S(1)}, s32[]{:S(2)}) async-start(s8[6291456]{0:T(1024)(128)(4,1)} %bitcast.47), calls=%async_computation.6 | async-start | bytes 4194304 | tf_op jit(solution)/shard_map/while
  155.7 2.6 copy-start.2
  165.5 137.1 %all-to-all-start.3 = ((bf16[128,8,256]{2,1,0:T(8,128)(2,1)}), bf16[128,8,256]{2,1,0:T(8,128)(2,1)S(1)}, u32[]{:S(2)}, u32[]{:S(2)}) async-start(bf16[128,8,256]{2,1,0:T(8,128)(2,1)} %bitcast.15), calls=%async_computation.3 | async-start | bytes 1048576 | tf_op jit(solution)/shard_map/all_to_all | solution.py:130
  312.4 12.8 %copy-start.1 = (bf16[3072,256]{1,0:T(8,128)(2,1)S(1)}, bf16[3072,256]{1,0:T(8,128)(2,1)}, u32[]{:S(2)}) copy-start(bf16[3072,256]{1,0:T(8,128)(2,1)} %param.17) | copy-start | bytes 4718596
Sparse Core Ops, SparseCore 0:
  119.3 161.9 all-gather.2
